TPU v7x, 128 devices: a whole 4x4x4 slice. The times are simulated.
128 devices in a mesh: fsdp: 4 (over y_lo, core), ctx: 32 (over z, x, y_hi).
Axes of the slice: x: 4, y: 4 (y_hi: 2, y_lo: 2; y = y_hi * 2 + y_lo), z: 4, core: 2. Of those that a mesh axis runs over, the one named last changes fastest.
Arguments:
- tokens: bfloat16 [4, 8192, 8192], P('fsdp', 'ctx'), may hold values from -6 to 6
- projection: bfloat16 [8192, 1536], P(('fsdp', 'ctx')), may hold values from -0.0625 to 0.0625
- short_taps: float32 [3, 1536], replicated, may hold values from -3 to 3
- long_filters: float32 [32, 8192], P('ctx'), may hold values from -4 to 4
- cotangent: bfloat16 [4, 512, 8192], P('fsdp', None, 'ctx'), may hold values from -6 to 6
Outputs:
- gated: bfloat16 [4, 512, 8192], P('fsdp', None, 'ctx')
- token_grad: bfloat16 [4, 8192, 8192], P('fsdp', 'ctx')
- filter_grad: float32 [32, 8192], P('ctx')
All inputs are finite; a program needn't handle non-finite values.
Results may differ from a plain program's by a relative error of at most 0.015.
Values may be sent and summed in bfloat16 or wider, within the bound.
A program may use at most 128 MiB of HBM per device.

v0:
```python
import math

import jax
import jax.numpy as jnp
from jax import lax
from jax.experimental import pallas as pl
from jax.experimental.pallas import tpu as pltpu
from jax.sharding import PartitionSpec as P

MESH = pl.DeviceIdType.MESH
BF = jnp.bfloat16
F32 = jnp.float32
FULL = slice(None)
ORDERS = ((0, 1, 2), (1, 2, 0), (2, 0, 1))


def my_coords():
    f = lax.axis_index("fsdp")
    t = lax.axis_index("ctx")
    return f % 2, (t // 8, (t // 2) % 4, (t % 2) * 2 + f // 2)


def device_of(core, pos):
    z, x, y = pos
    return ((y % 2) * 2 + core, z * 8 + x * 2 + y // 2)


def moved(pos, axis, by):
    out = list(pos)
    out[axis] = (pos[axis] + by) % 4
    return tuple(out)


def shards(ref, part, core, pos, half=None):
    z, x, y = pos
    rows = FULL if half is None else pl.ds(half * 32, 32)
    yl = FULL if y is None else y % 2
    yh = FULL if y is None else y // 2
    z = FULL if z is None else z
    x = FULL if x is None else x
    return ref.at[part, yl, core, z, x, yh, rows, :]


class Gather:
    def __init__(self, w, own, send, recv, sib_send, sib_recv):
        self.w, self.own = w, own
        self.send, self.recv = send, recv
        self.sib_send, self.sib_recv = sib_send, sib_recv
        self.core, self.pos = my_coords()
        self.started = []

    def block(self, part, phase, at, half=None, core=None):
        order = ORDERS[part]
        pos = [None, None, None]
        for later in order[phase + 1 :]:
            pos[later] = self.pos[later]
        pos[order[phase]] = at
        return shards(self.w, part, self.core if core is None else core, pos, half)

    def copy(self, part, phase, kind, at, by, half=None):
        axis = ORDERS[part][phase]
        ref = self.block(part, phase, at, half)
        return pltpu.make_async_remote_copy(
            src_ref=ref,
            dst_ref=ref,
            send_sem=self.send.at[part, phase, kind],
            recv_sem=self.recv.at[part, phase, kind],
            device_id=device_of(self.core, moved(self.pos, axis, by)),
            device_id_type=MESH,
        )

    def go(self, c):
        c.start()
        self.started.append(c)

    def me(self, part, phase):
        return self.pos[ORDERS[part][phase]]

    def first(self, part, phase):
        m = self.me(part, phase)
        self.go(self.copy(part, phase, 0, m, 1))
        self.go(self.copy(part, phase, 1, m, -1))

    def forward(self, part, phase, kind):
        m = self.me(part, phase)
        by = 1 if kind == 0 else -1
        at = (m - by) % 4
        self.copy(part, phase, kind, at, by).wait_recv()
        self.go(self.copy(part, phase, 2 + kind, at, by, half=kind))

    def last(self, part, phase, kind):
        m = self.me(part, phase)
        self.copy(part, phase, 2 + kind, (m + 2) % 4, 1, half=kind).wait_recv()

    def sibling(self, part, kind, at, half=None, receive=False):
        core = 1 - self.core if receive else self.core
        ref = self.block(part, 2, at, half, core)
        return pltpu.make_async_remote_copy(
            src_ref=ref,
            dst_ref=ref,
            send_sem=self.sib_send.at[part, kind],
            recv_sem=self.sib_recv.at[part, kind],
            device_id=device_of(1 - self.core, self.pos),
            device_id_type=MESH,
        )

    def wait_sends(self):
        for c in self.started:
            c.wait_send()


DN_NT = (((1,), (1,)), ((), ()))
KK = 4


def lanes(shape):
    return lax.broadcasted_iota(jnp.int32, shape, len(shape) - 1)


def fill_toeplitz(h_ref, s_ref):
    @pl.loop(0, 32)
    def _(k):
        now = h_ref[:, pl.ds(pl.multiple_of(256 * k, 256), 256)]
        earlier = jnp.maximum(k - 1, 0)
        before = h_ref[:, pl.ds(pl.multiple_of(256 * earlier, 256), 256)]
        before = jnp.where(k > 0, before, 0.0)
        row = jnp.concatenate([before, now], axis=1)
        base = pltpu.roll(jnp.broadcast_to(row, (8, 512)), 0, 1, stride=1, stride_axis=0)
        for b in range(8):
            one = base if b == 0 else pltpu.roll(base, 16 * b, 1)
            two = pltpu.roll(base, 16 * b + 8, 1)
            pair = jnp.concatenate([one, two], axis=0).astype(BF)
            s_ref[k, 16 * b : 16 * b + 16, :] = pair[:, 256:512]
            s_ref[k, 128 + 16 * b : 144 + 16 * b, :] = pair[:, 128:384]


def fill_taps(taps_ref, tap_ref, group):
    lane = lanes((16, 512))
    chan = lax.broadcasted_iota(jnp.int32, (16, 512), 0)
    pick = (lane == group * 16 + chan).astype(F32)
    for tap in range(3):
        for part in range(3):
            row = taps_ref[tap : tap + 1, 512 * part : 512 * part + 512]
            col = jnp.sum(pick * row, axis=1, keepdims=True)
            tap_ref[3 * tap + part] = jnp.broadcast_to(col, (16, 256))


def conv_front(x_ref, u_ref, tap_ref, wide_ref, mpad_ref, gpad_ref):
    lane = lanes((16, 256))
    mpad_ref[0:512, :] = jnp.zeros((512, 256), BF)
    gpad_ref[512:1024, :] = jnp.zeros((512, 256), BF)

    @pl.loop(0, 32)
    def _(a):
        prev = jnp.maximum(a - 1, 0)
        got = []
        for part in range(3):
            x = x_ref[part, a].astype(F32)
            y = x_ref[part, prev].astype(F32)
            y = jnp.where(a > 0, y, 0.0)
            one = jnp.where(lane < 1, pltpu.roll(y, 1, 1), pltpu.roll(x, 1, 1))
            two = jnp.where(lane < 2, pltpu.roll(y, 2, 1), pltpu.roll(x, 2, 1))
            short = tap_ref[part] * x + tap_ref[3 + part] * one + tap_ref[6 + part] * two
            wide_ref[part, a] = short
            got.append(short)
        rows = pl.ds(pl.multiple_of(16 * a, 16), 16)
        later = pl.ds(pl.multiple_of(512 + 16 * a, 16), 16)
        mpad_ref[later, :] = (got[1] * got[2]).astype(BF)
        gpad_ref[rows, :] = (u_ref[a].astype(F32) * got[0]).astype(BF)


def long_conv(mpad_ref, s_ref, acc_ref):
    acc_ref[...] = jnp.zeros_like(acc_ref)

    @pl.loop(0, 32 // KK)
    def _(n):
        lhs, rhs = [], []
        for i in range(KK):
            k = n * KK + i
            lhs.append(mpad_ref[pl.ds(pl.multiple_of(512 - 16 * k, 16), 512), :])
            rhs.append(s_ref[k])
        acc_ref[...] += jnp.dot(
            jnp.concatenate(lhs, axis=1), jnp.concatenate(rhs, axis=0), preferred_element_type=F32
        )


def long_back(gpad_ref, s_ref, acc_ref):
    acc_ref[...] = jnp.zeros_like(acc_ref)

    @pl.loop(0, 32 // KK)
    def _(n):
        lhs, rhs = [], []
        for i in range(KK):
            k = n * KK + i
            lhs.append(gpad_ref[pl.ds(pl.multiple_of(16 * k, 16), 512), :])
            rhs.append(s_ref[k])
        acc_ref[...] += lax.dot_general(
            jnp.concatenate(lhs, axis=1),
            jnp.concatenate(rhs, axis=1),
            DN_NT,
            preferred_element_type=F32,
        )


def gate_and_query_grad(acc_ref, u_ref, wide_ref, gated_ref, grad_ref):
    @pl.loop(0, 32)
    def _(a):
        rows = pl.ds(pl.multiple_of(16 * a, 16), 16)
        conv = acc_ref[rows, :].astype(BF).astype(F32)
        gated_ref[a] = (wide_ref[0, a] * conv).astype(BF)
        grad_ref[0, a] = u_ref[a].astype(F32) * conv


def back_taps(part, a, tap_ref, grad_ref, pg_ref):
    lane = lanes((16, 256))
    x = grad_ref[part, a]
    y = grad_ref[part, a + 1]
    one = jnp.where(lane > 254, pltpu.roll(y, 255, 1), pltpu.roll(x, 255, 1))
    two = jnp.where(lane > 253, pltpu.roll(y, 254, 1), pltpu.roll(x, 254, 1))
    out = tap_ref[part] * x + tap_ref[3 + part] * one + tap_ref[6 + part] * two
    pg_ref[part, a] = out.astype(BF)


def query_back(tap_ref, grad_ref, pg_ref):
    grad_ref[:, 32] = jnp.zeros((3, 16, 256), F32)

    @pl.loop(0, 32)
    def _(a):
        back_taps(0, a, tap_ref, grad_ref, pg_ref)


def key_value_back(acc_ref, wide_ref, tap_ref, grad_ref, pg_ref):
    @pl.loop(0, 32)
    def _(n):
        a = 31 - n
        rows = pl.ds(pl.multiple_of(16 * a, 16), 16)
        mg = acc_ref[rows, :].astype(BF).astype(F32)
        grad_ref[1, a] = mg * wide_ref[2, a]
        grad_ref[2, a] = mg * wide_ref[1, a]
        back_taps(1, a, tap_ref, grad_ref, pg_ref)
        back_taps(2, a, tap_ref, grad_ref, pg_ref)


def filter_back(mpad_ref, gpad_ref, mt_ref, z_ref, out_ref, kk=2):
    mt_ref[...] = mpad_ref[512:1024, :].astype(F32).T.astype(BF)
    z_ref[...] = jnp.zeros_like(z_ref)

    @pl.loop(0, 32 // kk)
    def _(n):
        for i in range(kk):
            k = n * kk + i
            q = jnp.dot(
                mt_ref[...],
                gpad_ref[pl.ds(pl.multiple_of(16 * k, 16), 512), :],
                preferred_element_type=F32,
            )
            top, low = q[0:128], q[128:256]
            x = jnp.concatenate(
                [jnp.zeros((128, 128), F32), low[:, 0:128], top[:, 0:128] + low[:, 128:256], top[:, 128:256]],
                axis=1,
            )
            for half in (64, 32, 16, 8):
                x = x[0:half] + pltpu.roll(x[half : 2 * half], 512 - half, 1)
            at = pl.ds(pl.multiple_of(256 * k, 256), 512)
            z_ref[:, at] += x
    x = z_ref[...]
    size = z_ref.shape[1]
    row = lax.broadcasted_iota(jnp.int32, x.shape, 0)
    for bit in (1, 2, 4):
        x = jnp.where(row // bit % 2 == 1, pltpu.roll(x, size - bit, 1), x)
    out_ref[...] = jnp.sum(x[:, 256:], axis=0, keepdims=True)


def each_peer(step):
    @pl.loop(1, 32)
    def _(d):
        step(d)


class Exchange:
    def __init__(self, src, dst, send, recv):
        self.src, self.dst, self.send, self.recv = src, dst, send, recv
        self.f, self.t = lax.axis_index("fsdp"), lax.axis_index("ctx")

    def copy(self, d):
        peer = (self.t + d) % 32
        return pltpu.make_async_remote_copy(
            src_ref=self.src(peer),
            dst_ref=self.dst(self.t),
            send_sem=self.send.at[d],
            recv_sem=self.recv.at[d],
            device_id=(self.f, peer),
            device_id_type=MESH,
        )

    def start(self):
        each_peer(lambda d: self.copy(d).start())

    def wait_recv(self):
        each_peer(lambda d: self.copy(d).wait_recv())

    def wait_send(self):
        each_peer(lambda d: self.copy(d).wait_send())


def project(part, near, pos, tok, w, acc):
    z, x, y = pos
    yl = y % 2

    @pl.loop(0, 8)
    def _(n):
        if part == 0:
            fy, fc, fz = (1 - yl if near else yl), n // 4, n % 4
        elif part == 1:
            fy, fc, fz = n // 4, n // 2 % 2, (z + n % 2 * 2 + near) % 4
        else:
            fy, fc, fz = n // 4, n // 2 % 2, n % 2 * 2
        row = (fy * 2 + fc) * 4 + fz
        if part < 2:
            lhs = tok[:, pl.ds(pl.multiple_of(row * 512, 512), 512)]
            rhs = w[part, fy, fc, fz].reshape(512, 512)
        else:
            left, right = [], []
            for i in range(2):
                for hop in (0, 2):
                    fx = (x + near + hop) % 4
                    at = pl.multiple_of(((row + i) * 4 + fx) * 128, 128)
                    left.append(tok[:, pl.ds(at, 128)])
                    right.append(w[part, fy, fc, fz + i, fx].reshape(128, 512))
            lhs = jnp.concatenate(left, axis=1)
            rhs = jnp.concatenate(right, axis=0)
        acc[part] += jnp.dot(lhs, rhs, preferred_element_type=F32)


def kernel(
    tok_hbm, own, taps, h, cot_hbm,
    gated_out, grad_out, filter_out,
    w, tok, acc3, p, x, u, s, tap, wide, mpad, gpad, acc, grad, pg, r, pgt, mt, z8, total, gated, fmine, fgot,
    put, send, recv, sib_send, sib_recv, local, a2a_send, a2a_recv, f_send, f_recv, out_sem,
):
    g = Gather(w, own, send, recv, sib_send, sib_recv)
    f, t = lax.axis_index("fsdp"), lax.axis_index("ctx")
    core, pos = g.core, g.pos
    barrier = pltpu.get_barrier_semaphore()

    def hello(device):
        pl.semaphore_signal(barrier, inc=1, device_id=device, device_id_type=MESH)

    each_peer(lambda d: hello((f, (t + d) % 32)))
    for d in range(1, 4):
        hello(((f + d) % 4, t))
    hello(((f + 2) % 4, t + 1 - t % 2 * 2))
    load = pltpu.make_async_copy(tok_hbm, tok, local.at[0])
    load.start()
    mine = []
    for part in range(3):
        c = pltpu.make_async_copy(
            own.at[:, pl.ds(512 * part, 512)], shards(w, part, core, pos), put.at[part]
        )
        c.start()
        mine.append(c)
    my_cot = pltpu.make_async_copy(cot_hbm.at[t], u.at[t], local.at[1])
    my_cot.start()
    for c in mine:
        c.wait()
    pl.semaphore_wait(barrier, 35)

    cots = Exchange(lambda q: cot_hbm.at[q], lambda q: u.at[q], a2a_send.at[0], a2a_recv.at[0])
    projs = Exchange(lambda q: p.at[:, q], lambda q: x.at[:, q], a2a_send.at[1], a2a_recv.at[1])
    gates = Exchange(lambda q: gated.at[q], lambda q: gated_out.at[q], a2a_send.at[2], a2a_recv.at[2])
    firsts = Exchange(lambda q: pg.at[0, q], lambda q: r.at[0, q], a2a_send.at[3], a2a_recv.at[3])
    others = Exchange(
        lambda q: pg.at[pl.ds(1, 2), q], lambda q: r.at[pl.ds(1, 2), q], a2a_send.at[4], a2a_recv.at[4]
    )

    for part in range(3):
        g.first(part, 0)
    fill_taps(taps, tap, t)
    acc3[...] = jnp.zeros_like(acc3)
    for phase in range(3):
        if phase == 2:
            cots.start()
            fill_toeplitz(h, s)
            load.wait()
        for kind in range(2):
            for part in range(3):
                g.forward(part, phase, kind)
                if phase == 2:
                    g.go(g.sibling(part, 1 + kind, (g.me(part, 2) + (-1, 1)[kind]) % 4))
        if phase == 2:
            for part in range(3):
                m = g.me(part, 2)
                g.sibling(part, 1, (m + 3) % 4, receive=True).wait_recv()
                g.sibling(part, 2, (m + 1) % 4, receive=True).wait_recv()
                project(part, 1, pos, tok, w, acc3)
        for part in range(3):
            for kind in range(2):
                g.last(part, phase, kind)
                if phase == 2:
                    g.go(g.sibling(part, 3 + kind, (g.me(part, 2) + 2) % 4, half=kind))
            if phase < 2:
                g.first(part, phase + 1)
            if phase == 1:
                g.go(g.sibling(part, 0, g.me(part, 2)))
    for part in range(3):
        m = g.me(part, 2)
        g.sibling(part, 0, m, receive=True).wait_recv()
        for kind in range(2):
            g.sibling(part, 3 + kind, (m + 2) % 4, half=kind, receive=True).wait_recv()
        project(part, 0, pos, tok, w, acc3)
        p[part] = acc3[part].T.astype(BF).reshape(32, 16, 256)
    projs.start()
    for part in range(3):
        x[part, t] = p[part, t]
    my_cot.wait()
    cots.wait_recv()
    projs.wait_recv()

    conv_front(x, u, tap, wide, mpad, gpad)
    long_conv(mpad, s, acc)
    gate_and_query_grad(acc, u, wide, gated, grad)
    gates.start()
    my_gate = pltpu.make_async_copy(gated.at[t], gated_out.at[t], local.at[2])
    my_gate.start()
    query_back(tap, grad, pg)
    firsts.start()
    r[0, t] = pg[0, t]
    long_back(gpad, s, acc)
    key_value_back(acc, wide, tap, grad, pg)
    others.start()
    for part in (1, 2):
        r[part, t] = pg[part, t]

    filter_back(mpad, gpad, mt, z8, fmine)
    shares = []
    for d in range(1, 4):
        c = pltpu.make_async_remote_copy(
            src_ref=fmine,
            dst_ref=fgot.at[d],
            send_sem=f_send.at[d],
            recv_sem=f_recv.at[d],
            device_id=((f + d) % 4, t),
            device_id_type=MESH,
        )
        c.start()
        shares.append(c)

    firsts.wait_recv()
    pgt[0] = r[0].reshape(512, 256).astype(F32).T.astype(BF)

    @pl.loop(0, 16)
    def _(n):
        rhs = w[0, n // 8, n // 4 % 2, n % 4].reshape(512, 512)
        total[n] = lax.dot_general(pgt[0], rhs, DN_NT, preferred_element_type=F32)

    for c in shares:
        c.wait_recv()
    scale = 1.0 / math.sqrt(4 * 16 * 8192)
    filter_out[...] = ((fmine[...] + fgot[1]) + (fgot[2] + fgot[3])) * scale

    others.wait_recv()
    for part in (1, 2):
        pgt[part] = r[part].reshape(512, 256).astype(F32).T.astype(BF)

    def store(n):
        at = pl.ds(pl.multiple_of(512 * n, 512), 512)
        return pltpu.make_async_copy(tok.at[:, at], grad_out.at[:, at], out_sem.at[n])

    @pl.loop(0, 16)
    def _(n):
        one = w[1, n // 8, n // 4 % 2, n % 4].reshape(512, 512)
        two = w[2, n // 8, n // 4 % 2, n % 4].reshape(512, 512)
        out = lax.dot_general(
            jnp.concatenate([pgt[1], pgt[2]], axis=1),
            jnp.concatenate([one, two], axis=1),
            DN_NT,
            preferred_element_type=F32,
        )
        tok[:, pl.ds(pl.multiple_of(512 * n, 512), 512)] = (total[n] + out).astype(BF)
        store(n).start()

    my_gate.wait()
    gates.wait_recv()
    for e in (cots, projs, gates, firsts, others):
        e.wait_send()
    for c in shares:
        c.wait_send()
    g.wait_sends()

    @pl.loop(0, 16)
    def _(n):
        store(n).wait()


def body(tokens, projection, short_taps, long_filters, cotangent):
    vmem = pl.BlockSpec(memory_space=pltpu.VMEM)
    hbm = pl.BlockSpec(memory_space=pl.ANY)
    dma = pltpu.SemaphoreType.DMA
    gated, token_grad, filter_grad = pl.pallas_call(
        kernel,
        out_shape=[
            jax.ShapeDtypeStruct((32, 16, 256), BF),
            jax.ShapeDtypeStruct((256, 8192), BF),
            jax.ShapeDtypeStruct((1, 8192), F32),
        ],
        in_specs=[hbm, vmem, vmem, vmem, hbm],
        out_specs=[hbm, hbm, vmem],
        scratch_shapes=[
            pltpu.VMEM((3, 2, 2, 4, 4, 2, 64, 512), BF),
            pltpu.VMEM((256, 8192), BF),
            pltpu.VMEM((3, 256, 512), F32),
            pltpu.VMEM((3, 32, 16, 256), BF),
            pltpu.VMEM((3, 32, 16, 256), BF),
            pltpu.VMEM((32, 16, 256), BF),
            pltpu.VMEM((32, 256, 256), BF),
            pltpu.VMEM((9, 16, 256), F32),
            pltpu.VMEM((3, 32, 16, 256), F32),
            pltpu.VMEM((1024, 256), BF),
            pltpu.VMEM((1024, 256), BF),
            pltpu.VMEM((512, 256), F32),
            pltpu.VMEM((3, 33, 16, 256), F32),
            pltpu.VMEM((3, 32, 16, 256), BF),
            pltpu.VMEM((3, 32, 16, 256), BF),
            pltpu.VMEM((3, 256, 512), BF),
            pltpu.VMEM((256, 512), BF),
            pltpu.VMEM((8, 8448), F32),
            pltpu.VMEM((16, 256, 512), F32),
            pltpu.VMEM((32, 16, 256), BF),
            pltpu.VMEM((1, 8192), F32),
            pltpu.VMEM((4, 1, 8192), F32),
            dma((3,)),
            dma((3, 3, 4)),
            dma((3, 3, 4)),
            dma((3, 5)),
            dma((3, 5)),
            dma((3,)),
            dma((5, 32)),
            dma((5, 32)),
            dma((4,)),
            dma((4,)),
            dma((16,)),
        ],
        compiler_params=pltpu.CompilerParams(
            collective_id=0, has_side_effects=True, vmem_limit_bytes=62 * 1024 * 1024
        ),
    )(tokens[0], projection, short_taps, long_filters, cotangent[0].reshape(32, 16, 256))
    return gated.reshape(1, 512, 256), token_grad[None], filter_grad


def solution(mesh):
    in_specs = (
        P("fsdp", "ctx", None),
        P(("fsdp", "ctx"), None),
        P(),
        P("ctx", None),
        P("fsdp", None, "ctx"),
    )
    out_specs = (P("fsdp", None, "ctx"), P("fsdp", "ctx", None), P("ctx", None))
    return jax.shard_map(body, mesh=mesh, in_specs=in_specs, out_specs=out_specs, check_vma=False)
```

profile of v0, /device:TPU:0, one launch (start us, length us, event | category | flops | bytes accessed | tf_op | source)
XLA Modules:
  0.0 147.6 jit_solution(10415773943721855118)
XLA Ops:
  0.6 140.0 %shard_map.76 = (bf16[32,16,256]{2,1,0:T(8,128)(2,1)}, bf16[256,8192]{1,0:T(8,128)(2,1)}, f32[1,8192]{1,0:T(1,128)}) custom-call(bf16[256,8192]{1,0:T(8,128)(2,1)} %bitcast.4, bf16[64,1536]{1,0:T(8,128)(2,1)} %own.1, f32[3,1536]{1,0:T(4,128)} %taps.1, f32[1,8192]{1,0:T(1,128)} %h.1, bf16[32,16,256]{2,1,0:T(8,128)(2,1)} %bitcast.6), custom_call_target="tpu_custom_call" | custom-call | tf_op jit(solution)/shard_map/pallas_call | solution.py:499
  140.6 1.7 %copy.11 = bf16[1,512,256]{2,1,0:T(8,128)(2,1)} copy(bf16[1,512,256]{2,1,0:T(8,128)(2,1)} %bitcast.7) | data formatting | bytes 524288
  142.3 0.0 copy-start
  142.3 4.6 %copy.12 = bf16[1,256,8192]{2,1,0:T(8,128)(2,1)} copy(bf16[1,256,8192]{2,1,0:T(8,128)(2,1)} %bitcast.5) | data formatting | bytes 8388608
  147.0 0.0 copy-done
  147.0 0.6 copy.13
Async XLA Ops:
  142.3 4.6 %copy-start = (f32[1,8192]{1,0:T(1,128)S(1)}, f32[1,8192]{1,0:T(1,128)}, u32[]{:S(2)}) copy-start(f32[1,8192]{1,0:T(1,128)} %get-tuple-element.14) | copy-start | bytes 98308
where the time goes:
time: 148 us
  Pallas kernels  140 us (95%)
  local copies, waits for them, and re-layouts  6.93 us (5%)
    pallas_call x1, Pallas kernels, body(): pl.pallas_call(kernel, out_shape=[jax.ShapeDtypeStruct((32, 16, 256), BF)...  140 us
    unnamed x5, local copies, waits for them, and re-layouts  6.93 us

commit v1 on v0

--- a/solution.py
+++ b/solution.py
@@ -11,6 +11,7 @@
 BF = jnp.bfloat16
 F32 = jnp.float32
 FULL = slice(None)
+SUBS = (0, 3, 1, 2)
 ORDERS = ((0, 1, 2), (1, 2, 0), (2, 0, 1))
 
 
@@ -49,22 +50,25 @@
         self.core, self.pos = my_coords()
         self.started = []
 
-    def block(self, part, phase, at, half=None, core=None):
+    def block(self, part, phase, at, half=None, core=None, sub=None):
         order = ORDERS[part]
         pos = [None, None, None]
         for later in order[phase + 1 :]:
             pos[later] = self.pos[later]
         pos[order[phase]] = at
+        if sub is not None:
+            pos[order[1]] = (self.pos[order[1]] + sub) % 4
         return shards(self.w, part, self.core if core is None else core, pos, half)
 
-    def copy(self, part, phase, kind, at, by, half=None):
+    def copy(self, part, phase, kind, at, by, half=None, sub=None):
         axis = ORDERS[part][phase]
-        ref = self.block(part, phase, at, half)
+        ref = self.block(part, phase, at, half, sub=sub)
+        at = (part, phase, kind) if sub is None else (part, 2 + sub, kind)
         return pltpu.make_async_remote_copy(
             src_ref=ref,
             dst_ref=ref,
-            send_sem=self.send.at[part, phase, kind],
-            recv_sem=self.recv.at[part, phase, kind],
+            send_sem=self.send.at[at],
+            recv_sem=self.recv.at[at],
             device_id=device_of(self.core, moved(self.pos, axis, by)),
             device_id_type=MESH,
         )
@@ -76,41 +80,51 @@
     def me(self, part, phase):
         return self.pos[ORDERS[part][phase]]
 
-    def first(self, part, phase):
+    def first(self, part, phase, sub=None):
         m = self.me(part, phase)
-        self.go(self.copy(part, phase, 0, m, 1))
-        self.go(self.copy(part, phase, 1, m, -1))
-
-    def forward(self, part, phase, kind):
+        self.go(self.copy(part, phase, 0, m, 1, sub=sub))
+        self.go(self.copy(part, phase, 1, m, -1, sub=sub))
+
+    def forward(self, part, phase, kind, sub=None):
         m = self.me(part, phase)
         by = 1 if kind == 0 else -1
         at = (m - by) % 4
-        self.copy(part, phase, kind, at, by).wait_recv()
-        self.go(self.copy(part, phase, 2 + kind, at, by, half=kind))
-
-    def last(self, part, phase, kind):
+        self.copy(part, phase, kind, at, by, sub=sub).wait_recv()
+        self.go(self.copy(part, phase, 2 + kind, at, by, half=kind, sub=sub))
+        if phase == 2:
+            self.go(self.sibling(part, 1 + kind, sub))
+
+    def last(self, part, phase, kind, sub=None):
         m = self.me(part, phase)
-        self.copy(part, phase, 2 + kind, (m + 2) % 4, 1, half=kind).wait_recv()
-
-    def sibling(self, part, kind, at, half=None, receive=False):
+        self.copy(part, phase, 2 + kind, (m + 2) % 4, 1, half=kind, sub=sub).wait_recv()
+        if phase == 2:
+            self.go(self.sibling(part, 3 + kind, sub))
+
+    def sibling(self, part, kind, sub, receive=False):
         core = 1 - self.core if receive else self.core
-        ref = self.block(part, 2, at, half, core)
+        at = (self.me(part, 2) + (0, -1, 1, 2, 2)[kind]) % 4
+        ref = self.block(part, 2, at, None if kind < 3 else kind - 3, core, sub)
         return pltpu.make_async_remote_copy(
             src_ref=ref,
             dst_ref=ref,
-            send_sem=self.sib_send.at[part, kind],
-            recv_sem=self.sib_recv.at[part, kind],
+            send_sem=self.sib_send.at[part, sub, kind],
+            recv_sem=self.sib_recv.at[part, sub, kind],
             device_id=device_of(1 - self.core, self.pos),
             device_id_type=MESH,
         )
 
+    def from_sibling(self, part, kinds):
+        for sub in range(4):
+            for kind in kinds:
+                self.sibling(part, kind, sub, receive=True).wait_recv()
+
     def wait_sends(self):
         for c in self.started:
             c.wait_send()
 
 
 DN_NT = (((1,), (1,)), ((), ()))
-KK = 4
+KK = 8
 
 
 def lanes(shape):
@@ -118,7 +132,7 @@
 
 
 def fill_toeplitz(h_ref, s_ref):
-    @pl.loop(0, 32)
+    @pl.loop(0, 32, unroll=2)
     def _(k):
         now = h_ref[:, pl.ds(pl.multiple_of(256 * k, 256), 256)]
         earlier = jnp.maximum(k - 1, 0)
@@ -150,7 +164,7 @@
     mpad_ref[0:512, :] = jnp.zeros((512, 256), BF)
     gpad_ref[512:1024, :] = jnp.zeros((512, 256), BF)
 
-    @pl.loop(0, 32)
+    @pl.loop(0, 32, unroll=4)
     def _(a):
         prev = jnp.maximum(a - 1, 0)
         got = []
@@ -170,40 +184,33 @@
 
 
 def long_conv(mpad_ref, s_ref, acc_ref):
-    acc_ref[...] = jnp.zeros_like(acc_ref)
-
-    @pl.loop(0, 32 // KK)
-    def _(n):
-        lhs, rhs = [], []
-        for i in range(KK):
-            k = n * KK + i
-            lhs.append(mpad_ref[pl.ds(pl.multiple_of(512 - 16 * k, 16), 512), :])
-            rhs.append(s_ref[k])
-        acc_ref[...] += jnp.dot(
-            jnp.concatenate(lhs, axis=1), jnp.concatenate(rhs, axis=0), preferred_element_type=F32
+    for n in range(32 // KK):
+        low = 16 * KK * n
+        lhs = [mpad_ref[512 + low - 16 * k : 1024 - 16 * k, :] for k in range(n * KK, n * KK + KK)]
+        rhs = s_ref[n * KK : n * KK + KK].reshape(256 * KK, 256)
+        out = jnp.dot(jnp.concatenate(lhs, axis=1), rhs, preferred_element_type=F32)
+        if n == 0:
+            acc_ref[...] = out
+        else:
+            acc_ref[low:512, :] += out
+
+
+def long_back(gpad_ref, s_ref, acc_ref):
+    for n in range(32 // KK):
+        high = 512 - 16 * KK * n
+        lhs = [gpad_ref[16 * k : 16 * k + high, :] for k in range(n * KK, n * KK + KK)]
+        rhs = [s_ref[k] for k in range(n * KK, n * KK + KK)]
+        out = lax.dot_general(
+            jnp.concatenate(lhs, axis=1), jnp.concatenate(rhs, axis=1), DN_NT, preferred_element_type=F32
         )
-
-
-def long_back(gpad_ref, s_ref, acc_ref):
-    acc_ref[...] = jnp.zeros_like(acc_ref)
-
-    @pl.loop(0, 32 // KK)
-    def _(n):
-        lhs, rhs = [], []
-        for i in range(KK):
-            k = n * KK + i
-            lhs.append(gpad_ref[pl.ds(pl.multiple_of(16 * k, 16), 512), :])
-            rhs.append(s_ref[k])
-        acc_ref[...] += lax.dot_general(
-            jnp.concatenate(lhs, axis=1),
-            jnp.concatenate(rhs, axis=1),
-            DN_NT,
-            preferred_element_type=F32,
-        )
+        if n == 0:
+            acc_ref[...] = out
+        else:
+            acc_ref[0:high, :] += out
 
 
 def gate_and_query_grad(acc_ref, u_ref, wide_ref, gated_ref, grad_ref):
-    @pl.loop(0, 32)
+    @pl.loop(0, 32, unroll=4)
     def _(a):
         rows = pl.ds(pl.multiple_of(16 * a, 16), 16)
         conv = acc_ref[rows, :].astype(BF).astype(F32)
@@ -224,51 +231,55 @@
 def query_back(tap_ref, grad_ref, pg_ref):
     grad_ref[:, 32] = jnp.zeros((3, 16, 256), F32)
 
-    @pl.loop(0, 32)
+    @pl.loop(0, 32, unroll=4)
     def _(a):
         back_taps(0, a, tap_ref, grad_ref, pg_ref)
 
 
 def key_value_back(acc_ref, wide_ref, tap_ref, grad_ref, pg_ref):
-    @pl.loop(0, 32)
-    def _(n):
-        a = 31 - n
+    @pl.loop(0, 32, unroll=4)
+    def _(a):
         rows = pl.ds(pl.multiple_of(16 * a, 16), 16)
         mg = acc_ref[rows, :].astype(BF).astype(F32)
         grad_ref[1, a] = mg * wide_ref[2, a]
         grad_ref[2, a] = mg * wide_ref[1, a]
+
+    @pl.loop(0, 32, unroll=4)
+    def _(a):
         back_taps(1, a, tap_ref, grad_ref, pg_ref)
         back_taps(2, a, tap_ref, grad_ref, pg_ref)
 
 
-def filter_back(mpad_ref, gpad_ref, mt_ref, z_ref, out_ref, kk=2):
+def filter_back(mpad_ref, gpad_ref, mt_ref, z_ref, out_ref):
     mt_ref[...] = mpad_ref[512:1024, :].astype(F32).T.astype(BF)
-    z_ref[...] = jnp.zeros_like(z_ref)
-
-    @pl.loop(0, 32 // kk)
-    def _(n):
-        for i in range(kk):
-            k = n * kk + i
-            q = jnp.dot(
-                mt_ref[...],
-                gpad_ref[pl.ds(pl.multiple_of(16 * k, 16), 512), :],
-                preferred_element_type=F32,
-            )
-            top, low = q[0:128], q[128:256]
-            x = jnp.concatenate(
-                [jnp.zeros((128, 128), F32), low[:, 0:128], top[:, 0:128] + low[:, 128:256], top[:, 128:256]],
-                axis=1,
-            )
-            for half in (64, 32, 16, 8):
-                x = x[0:half] + pltpu.roll(x[half : 2 * half], 512 - half, 1)
-            at = pl.ds(pl.multiple_of(256 * k, 256), 512)
-            z_ref[:, at] += x
-    x = z_ref[...]
-    size = z_ref.shape[1]
-    row = lax.broadcasted_iota(jnp.int32, x.shape, 0)
-    for bit in (1, 2, 4):
-        x = jnp.where(row // bit % 2 == 1, pltpu.roll(x, size - bit, 1), x)
-    out_ref[...] = jnp.sum(x[:, 256:], axis=0, keepdims=True)
+    for n in range(32 // KK):
+        deep = 512 - 16 * KK * n
+
+        @pl.loop(n * KK // 4, n * KK // 4 + KK // 4)
+        def _(m):
+            four = [gpad_ref[pl.ds(pl.multiple_of(64 * m + 16 * i, 16), deep), :] for i in range(4)]
+            wide = jnp.dot(mt_ref[:, 0:deep], jnp.concatenate(four, axis=1), preferred_element_type=F32)
+            for i in range(4):
+                q = wide[:, 256 * i : 256 * i + 256]
+                top, low = q[0:128], q[128:256]
+                mid = top[:, 0:128] + low[:, 128:256]
+                blank = jnp.zeros((128, 128), F32)
+                x = jnp.concatenate([blank, low[:, 0:128], mid, top[:, 128:256]], axis=1)
+                for half in (64, 32, 16, 8):
+                    x = x[0:half] + pltpu.roll(x[half : 2 * half], 512 - half, 1)
+                z_ref[4 * m + i] = x
+
+    for k in range(32):
+        x = z_ref[k, :, 256:512]
+        y = z_ref[k + 1, :, 0:256] if k < 31 else jnp.zeros((8, 256), F32)
+        after = z_ref[k + 1, :, 256:512] if k < 31 else jnp.zeros((8, 256), F32)
+        if k < 30:
+            after += z_ref[k + 2, :, 0:256]
+        x = jnp.concatenate([x + y, after], axis=1)
+        row = lax.broadcasted_iota(jnp.int32, x.shape, 0)
+        for bit in (1, 2, 4):
+            x = jnp.where(row // bit % 2 == 1, pltpu.roll(x, 512 - bit, 1), x)
+        out_ref[:, 256 * k : 256 * k + 256] = jnp.sum(x[:, 0:256], axis=0, keepdims=True)
 
 
 def each_peer(step):
@@ -305,37 +316,34 @@
 
 def project(part, near, pos, tok, w, acc):
     z, x, y = pos
-    yl = y % 2
-
-    @pl.loop(0, 8)
-    def _(n):
+    for n in range(2):
+        left, right = [], []
+
+        def piece(row, size, block):
+            left.append(tok[:, pl.ds(pl.multiple_of(row * size, size), size)])
+            right.append(block.reshape(size, 512))
+
         if part == 0:
-            fy, fc, fz = (1 - yl if near else yl), n // 4, n % 4
-        elif part == 1:
-            fy, fc, fz = n // 4, n // 2 % 2, (z + n % 2 * 2 + near) % 4
+            fy = (y + near) % 2
+            piece(fy * 2 + n, 2048, w[part, fy, n])
         else:
-            fy, fc, fz = n // 4, n // 2 % 2, n % 2 * 2
-        row = (fy * 2 + fc) * 4 + fz
-        if part < 2:
-            lhs = tok[:, pl.ds(pl.multiple_of(row * 512, 512), 512)]
-            rhs = w[part, fy, fc, fz].reshape(512, 512)
-        else:
-            left, right = [], []
-            for i in range(2):
+            for fc in range(2):
                 for hop in (0, 2):
-                    fx = (x + near + hop) % 4
-                    at = pl.multiple_of(((row + i) * 4 + fx) * 128, 128)
-                    left.append(tok[:, pl.ds(at, 128)])
-                    right.append(w[part, fy, fc, fz + i, fx].reshape(128, 512))
-            lhs = jnp.concatenate(left, axis=1)
-            rhs = jnp.concatenate(right, axis=0)
-        acc[part] += jnp.dot(lhs, rhs, preferred_element_type=F32)
+                    if part == 1:
+                        fz = (z + near + hop) % 4
+                        piece((n * 2 + fc) * 4 + fz, 512, w[part, n, fc, fz])
+                    else:
+                        fx = (x + near + hop) % 4
+                        for fz in range(4):
+                            piece(((n * 2 + fc) * 4 + fz) * 4 + fx, 128, w[part, n, fc, fz, fx])
+        lhs = jnp.concatenate(left, axis=1)
+        acc[part] += jnp.dot(lhs, jnp.concatenate(right, axis=0), preferred_element_type=F32)
 
 
 def kernel(
     tok_hbm, own, taps, h, cot_hbm,
     gated_out, grad_out, filter_out,
-    w, tok, acc3, p, x, u, s, tap, wide, mpad, gpad, acc, grad, pg, r, pgt, mt, z8, total, gated, fmine, fgot,
+    w, tok, acc3, p, x, u, s, tap, wide, mpad, gpad, acc, grad, pg, r, mt, z8, total, gated, fmine, fgot,
     put, send, recv, sib_send, sib_recv, local, a2a_send, a2a_recv, f_send, f_recv, out_sem,
 ):
     g = Gather(w, own, send, recv, sib_send, sib_recv)
@@ -373,40 +381,53 @@
         lambda q: pg.at[pl.ds(1, 2), q], lambda q: r.at[pl.ds(1, 2), q], a2a_send.at[4], a2a_recv.at[4]
     )
 
-    for part in range(3):
+    parts = range(3)
+    for part in parts:
         g.first(part, 0)
     fill_taps(taps, tap, t)
     acc3[...] = jnp.zeros_like(acc3)
-    for phase in range(3):
-        if phase == 2:
-            cots.start()
-            fill_toeplitz(h, s)
-            load.wait()
+    for kind in range(2):
+        for part in parts:
+            g.forward(part, 0, kind)
+    for part in parts:
         for kind in range(2):
-            for part in range(3):
-                g.forward(part, phase, kind)
-                if phase == 2:
-                    g.go(g.sibling(part, 1 + kind, (g.me(part, 2) + (-1, 1)[kind]) % 4))
-        if phase == 2:
-            for part in range(3):
-                m = g.me(part, 2)
-                g.sibling(part, 1, (m + 3) % 4, receive=True).wait_recv()
-                g.sibling(part, 2, (m + 1) % 4, receive=True).wait_recv()
-                project(part, 1, pos, tok, w, acc3)
-        for part in range(3):
+            g.last(part, 0, kind)
+        g.first(part, 1)
+        g.first(part, 2, 0)
+        g.go(g.sibling(part, 0, 0))
+    for kind in range(2):
+        for part in parts:
+            g.forward(part, 1, kind)
+            g.first(part, 2, SUBS[1 + kind])
+            g.go(g.sibling(part, 0, SUBS[1 + kind]))
+    for part in parts:
+        for kind in range(2):
+            g.last(part, 1, kind)
+        g.first(part, 2, 2)
+        g.go(g.sibling(part, 0, 2))
+    fill_toeplitz(h, s)
+    for kind in range(2):
+        for part in parts:
+            g.forward(part, 2, kind, 0)
+    cots.start()
+    load.wait()
+    for sub in SUBS[1:]:
+        for kind in range(2):
+            for part in parts:
+                g.forward(part, 2, kind, sub)
+    for sub in SUBS[:2]:
+        for part in parts:
             for kind in range(2):
-                g.last(part, phase, kind)
-                if phase == 2:
-                    g.go(g.sibling(part, 3 + kind, (g.me(part, 2) + 2) % 4, half=kind))
-            if phase < 2:
-                g.first(part, phase + 1)
-            if phase == 1:
-                g.go(g.sibling(part, 0, g.me(part, 2)))
-    for part in range(3):
-        m = g.me(part, 2)
-        g.sibling(part, 0, m, receive=True).wait_recv()
-        for kind in range(2):
-            g.sibling(part, 3 + kind, (m + 2) % 4, half=kind, receive=True).wait_recv()
+                g.last(part, 2, kind, sub)
+    for part in parts:
+        g.from_sibling(part, (1, 2))
+        project(part, 1, pos, tok, w, acc3)
+    for sub in SUBS[2:]:
+        for part in parts:
+            for kind in range(2):
+                g.last(part, 2, kind, sub)
+    for part in parts:
+        g.from_sibling(part, (0, 3, 4))
         project(part, 0, pos, tok, w, acc3)
         p[part] = acc3[part].T.astype(BF).reshape(32, 16, 256)
     projs.start()
@@ -445,13 +466,14 @@
         c.start()
         shares.append(c)
 
+    def weights(part, n):
+        return w[part, n // 4, n // 2 % 2, pl.ds(n % 2 * 2, 2)].reshape(1024, 512)
+
     firsts.wait_recv()
-    pgt[0] = r[0].reshape(512, 256).astype(F32).T.astype(BF)
-
-    @pl.loop(0, 16)
+
+    @pl.loop(0, 8)
     def _(n):
-        rhs = w[0, n // 8, n // 4 % 2, n % 4].reshape(512, 512)
-        total[n] = lax.dot_general(pgt[0], rhs, DN_NT, preferred_element_type=F32)
+        total[n] = jnp.dot(weights(0, n), r[0].reshape(512, 256), preferred_element_type=F32)
 
     for c in shares:
         c.wait_recv()
@@ -459,24 +481,16 @@
     filter_out[...] = ((fmine[...] + fgot[1]) + (fgot[2] + fgot[3])) * scale
 
     others.wait_recv()
-    for part in (1, 2):
-        pgt[part] = r[part].reshape(512, 256).astype(F32).T.astype(BF)
 
     def store(n):
-        at = pl.ds(pl.multiple_of(512 * n, 512), 512)
+        at = pl.ds(pl.multiple_of(1024 * n, 1024), 1024)
         return pltpu.make_async_copy(tok.at[:, at], grad_out.at[:, at], out_sem.at[n])
 
-    @pl.loop(0, 16)
+    @pl.loop(0, 8)
     def _(n):
-        one = w[1, n // 8, n // 4 % 2, n % 4].reshape(512, 512)
-        two = w[2, n // 8, n // 4 % 2, n % 4].reshape(512, 512)
-        out = lax.dot_general(
-            jnp.concatenate([pgt[1], pgt[2]], axis=1),
-            jnp.concatenate([one, two], axis=1),
-            DN_NT,
-            preferred_element_type=F32,
-        )
-        tok[:, pl.ds(pl.multiple_of(512 * n, 512), 512)] = (total[n] + out).astype(BF)
+        lhs = jnp.concatenate([weights(1, n), weights(2, n)], axis=1)
+        out = total[n] + jnp.dot(lhs, r[1:3].reshape(1024, 256), preferred_element_type=F32)
+        tok[:, pl.ds(pl.multiple_of(1024 * n, 1024), 1024)] = out.astype(BF).T
         store(n).start()
 
     my_gate.wait()
@@ -487,7 +501,7 @@
         c.wait_send()
     g.wait_sends()
 
-    @pl.loop(0, 16)
+    @pl.loop(0, 8)
     def _(n):
         store(n).wait()
 
@@ -521,24 +535,23 @@
             pltpu.VMEM((3, 33, 16, 256), F32),
             pltpu.VMEM((3, 32, 16, 256), BF),
             pltpu.VMEM((3, 32, 16, 256), BF),
-            pltpu.VMEM((3, 256, 512), BF),
             pltpu.VMEM((256, 512), BF),
-            pltpu.VMEM((8, 8448), F32),
-            pltpu.VMEM((16, 256, 512), F32),
+            pltpu.VMEM((32, 8, 512), F32),
+            pltpu.VMEM((8, 1024, 256), F32),
             pltpu.VMEM((32, 16, 256), BF),
             pltpu.VMEM((1, 8192), F32),
             pltpu.VMEM((4, 1, 8192), F32),
             dma((3,)),
-            dma((3, 3, 4)),
-            dma((3, 3, 4)),
-            dma((3, 5)),
-            dma((3, 5)),
+            dma((3, 6, 4)),
+            dma((3, 6, 4)),
+            dma((3, 4, 5)),
+            dma((3, 4, 5)),
             dma((3,)),
             dma((5, 32)),
             dma((5, 32)),
             dma((4,)),
             dma((4,)),
-            dma((16,)),
+            dma((8,)),
         ],
         compiler_params=pltpu.CompilerParams(
             collective_id=0, has_side_effects=True, vmem_limit_bytes=62 * 1024 * 1024

time: 148 us -> 126 us (0.85); the launches traced: 148 us -> 124 us
  Pallas kernels: 140 us -> 116 us
    pallas_call x1, Pallas kernels: 140 us -> 116 us  [body(): pl.pallas_call(kernel, out_shape=[jax.ShapeDtypeStruct((32, 16, 256), BF)...]
where the time goes in v1:
time: 126 us; the launch traced here: 124 us
  Pallas kernels  116 us (92%)
  local copies, waits for them, and re-layouts  6.93 us (6%)
    pallas_call x1, Pallas kernels, body(): pl.pallas_call(kernel, out_shape=[jax.ShapeDtypeStruct((32, 16, 256), BF)...  116 us
    unnamed x5, local copies, waits for them, and re-layouts  6.93 us

profile of v1, /device:TPU:0, one launch (start us, length us, event | category | flops | bytes accessed | tf_op | source)
XLA Modules:
  0.0 123.9 jit_solution(12160851717006375818)
XLA Ops:
  0.6 116.3 %shard_map.76 = (bf16[32,16,256]{2,1,0:T(8,128)(2,1)}, bf16[256,8192]{1,0:T(8,128)(2,1)}, f32[1,8192]{1,0:T(1,128)}) custom-call(bf16[256,8192]{1,0:T(8,128)(2,1)} %bitcast.4, bf16[64,1536]{1,0:T(8,128)(2,1)} %own.1, f32[3,1536]{1,0:T(4,128)} %taps.1, f32[1,8192]{1,0:T(1,128)} %h.1, bf16[32,16,256]{2,1,0:T(8,128)(2,1)} %bitcast.6), custom_call_target="tpu_custom_call" | custom-call | tf_op jit(solution)/shard_map/pallas_call | solution.py:513
  117.0 1.7 %copy.11 = bf16[1,512,256]{2,1,0:T(8,128)(2,1)} copy(bf16[1,512,256]{2,1,0:T(8,128)(2,1)} %bitcast.7) | data formatting | bytes 524288
  118.6 0.0 copy-start
  118.6 4.6 %copy.12 = bf16[1,256,8192]{2,1,0:T(8,128)(2,1)} copy(bf16[1,256,8192]{2,1,0:T(8,128)(2,1)} %bitcast.5) | data formatting | bytes 8388608
  123.3 0.0 copy-done
  123.3 0.6 copy.13
Async XLA Ops:
  118.6 4.6 %copy-start = (f32[1,8192]{1,0:T(1,128)S(1)}, f32[1,8192]{1,0:T(1,128)}, u32[]{:S(2)}) copy-start(f32[1,8192]{1,0:T(1,128)} %get-tuple-element.14) | copy-start | bytes 98308

commit v2 on v1

--- a/solution.py
+++ b/solution.py
@@ -113,8 +113,8 @@
             device_id_type=MESH,
         )
 
-    def from_sibling(self, part, kinds):
-        for sub in range(4):
+    def from_sibling(self, part, kinds, subs):
+        for sub in subs:
             for kind in kinds:
                 self.sibling(part, kind, sub, receive=True).wait_recv()
 
@@ -229,14 +229,14 @@
 
 
 def query_back(tap_ref, grad_ref, pg_ref):
-    grad_ref[:, 32] = jnp.zeros((3, 16, 256), F32)
-
     @pl.loop(0, 32, unroll=4)
     def _(a):
         back_taps(0, a, tap_ref, grad_ref, pg_ref)
 
 
 def key_value_back(acc_ref, wide_ref, tap_ref, grad_ref, pg_ref):
+    grad_ref[:, 32] = jnp.zeros((3, 16, 256), F32)
+
     @pl.loop(0, 32, unroll=4)
     def _(a):
         rows = pl.ds(pl.multiple_of(16 * a, 16), 16)
@@ -282,8 +282,8 @@
         out_ref[:, 256 * k : 256 * k + 256] = jnp.sum(x[:, 0:256], axis=0, keepdims=True)
 
 
-def each_peer(step):
-    @pl.loop(1, 32)
+def each_peer(step, unroll=1):
+    @pl.loop(1, 32, unroll=unroll)
     def _(d):
         step(d)
 
@@ -305,7 +305,7 @@
         )
 
     def start(self):
-        each_peer(lambda d: self.copy(d).start())
+        each_peer(lambda d: self.copy(d).start(), 31)
 
     def wait_recv(self):
         each_peer(lambda d: self.copy(d).wait_recv())
@@ -314,30 +314,40 @@
         each_peer(lambda d: self.copy(d).wait_send())
 
 
-def project(part, near, pos, tok, w, acc):
+def project(part, near, subs, pos, tok, w, acc):
     z, x, y = pos
-    for n in range(2):
-        left, right = [], []
-
-        def piece(row, size, block):
-            left.append(tok[:, pl.ds(pl.multiple_of(row * size, size), size)])
-            right.append(block.reshape(size, 512))
-
+    left, right = [], []
+
+    def piece(row, size, block):
+        left.append(tok[:, pl.ds(pl.multiple_of(row * size, size), size)])
+        right.append(block.reshape(size, 512))
+
+    for fc in range(2):
         if part == 0:
             fy = (y + near) % 2
-            piece(fy * 2 + n, 2048, w[part, fy, n])
-        else:
-            for fc in range(2):
-                for hop in (0, 2):
-                    if part == 1:
-                        fz = (z + near + hop) % 4
-                        piece((n * 2 + fc) * 4 + fz, 512, w[part, n, fc, fz])
-                    else:
-                        fx = (x + near + hop) % 4
-                        for fz in range(4):
-                            piece(((n * 2 + fc) * 4 + fz) * 4 + fx, 128, w[part, n, fc, fz, fx])
-        lhs = jnp.concatenate(left, axis=1)
-        acc[part] += jnp.dot(lhs, jnp.concatenate(right, axis=0), preferred_element_type=F32)
+            if len(subs) == 4:
+                piece(fy * 2 + fc, 2048, w[part, fy, fc])
+            else:
+                for sub in subs:
+                    fx = (x + sub) % 4
+                    for fz in range(4):
+                        piece(((fy * 2 + fc) * 4 + fz) * 4 + fx, 128, w[part, fy, fc, fz, fx])
+        for hop in (0, 2):
+            if part == 1:
+                fz = (z + near + hop) % 4
+                for sub in subs:
+                    if sub < 2:
+                        fy = (y + sub) % 2
+                        piece((fy * 2 + fc) * 4 + fz, 512, w[part, fy, fc, fz])
+            if part == 2:
+                fx = (x + near + hop) % 4
+                for fy in range(2):
+                    for sub in subs:
+                        fz = (z + sub) % 4
+                        piece(((fy * 2 + fc) * 4 + fz) * 4 + fx, 128, w[part, fy, fc, fz, fx])
+    acc[part] += jnp.dot(
+        jnp.concatenate(left, axis=1), jnp.concatenate(right, axis=0), preferred_element_type=F32
+    )
 
 
 def kernel(
@@ -354,10 +364,10 @@
     def hello(device):
         pl.semaphore_signal(barrier, inc=1, device_id=device, device_id_type=MESH)
 
-    each_peer(lambda d: hello((f, (t + d) % 32)))
-    for d in range(1, 4):
-        hello(((f + d) % 4, t))
-    hello(((f + 2) % 4, t + 1 - t % 2 * 2))
+    for axis in range(3):
+        for by in (1, -1):
+            hello(device_of(core, moved(pos, axis, by)))
+    hello(device_of(1 - core, pos))
     load = pltpu.make_async_copy(tok_hbm, tok, local.at[0])
     load.start()
     mine = []
@@ -371,7 +381,7 @@
     my_cot.start()
     for c in mine:
         c.wait()
-    pl.semaphore_wait(barrier, 35)
+    pl.semaphore_wait(barrier, 7)
 
     cots = Exchange(lambda q: cot_hbm.at[q], lambda q: u.at[q], a2a_send.at[0], a2a_recv.at[0])
     projs = Exchange(lambda q: p.at[:, q], lambda q: x.at[:, q], a2a_send.at[1], a2a_recv.at[1])
@@ -409,26 +419,30 @@
     for kind in range(2):
         for part in parts:
             g.forward(part, 2, kind, 0)
-    cots.start()
     load.wait()
     for sub in SUBS[1:]:
         for kind in range(2):
             for part in parts:
                 g.forward(part, 2, kind, sub)
-    for sub in SUBS[:2]:
-        for part in parts:
-            for kind in range(2):
-                g.last(part, 2, kind, sub)
+    def lasts(subs):
+        for sub in subs:
+            for part in parts:
+                for kind in range(2):
+                    g.last(part, 2, kind, sub)
+
+    lasts(SUBS[:2])
     for part in parts:
-        g.from_sibling(part, (1, 2))
-        project(part, 1, pos, tok, w, acc3)
-    for sub in SUBS[2:]:
-        for part in parts:
-            for kind in range(2):
-                g.last(part, 2, kind, sub)
+        g.from_sibling(part, (1, 2), SUBS)
+        project(part, 1, SUBS, pos, tok, w, acc3)
+    lasts(SUBS[2:3])
+    for part in (1, 0, 2):
+        g.from_sibling(part, (0, 3, 4), SUBS[:3])
+        project(part, 0, SUBS[1:3] if part == 1 else SUBS[:3], pos, tok, w, acc3)
+    lasts(SUBS[3:])
+    cots.start()
     for part in parts:
-        g.from_sibling(part, (0, 3, 4))
-        project(part, 0, pos, tok, w, acc3)
+        g.from_sibling(part, (0, 3, 4), SUBS[3:])
+        project(part, 0, (0, 2) if part == 1 else SUBS[3:], pos, tok, w, acc3)
         p[part] = acc3[part].T.astype(BF).reshape(32, 16, 256)
     projs.start()
     for part in range(3):
@@ -438,19 +452,19 @@
     projs.wait_recv()
 
     conv_front(x, u, tap, wide, mpad, gpad)
-    long_conv(mpad, s, acc)
-    gate_and_query_grad(acc, u, wide, gated, grad)
-    gates.start()
-    my_gate = pltpu.make_async_copy(gated.at[t], gated_out.at[t], local.at[2])
-    my_gate.start()
-    query_back(tap, grad, pg)
-    firsts.start()
-    r[0, t] = pg[0, t]
     long_back(gpad, s, acc)
     key_value_back(acc, wide, tap, grad, pg)
     others.start()
     for part in (1, 2):
         r[part, t] = pg[part, t]
+    long_conv(mpad, s, acc)
+    gate_and_query_grad(acc, u, wide, gated, grad)
+    query_back(tap, grad, pg)
+    firsts.start()
+    r[0, t] = pg[0, t]
+    gates.start()
+    my_gate = pltpu.make_async_copy(gated.at[t], gated_out.at[t], local.at[2])
+    my_gate.start()
 
     filter_back(mpad, gpad, mt, z8, fmine)
     shares = []
@@ -469,18 +483,19 @@
     def weights(part, n):
         return w[part, n // 4, n // 2 % 2, pl.ds(n % 2 * 2, 2)].reshape(1024, 512)
 
-    firsts.wait_recv()
+    others.wait_recv()
 
     @pl.loop(0, 8)
     def _(n):
-        total[n] = jnp.dot(weights(0, n), r[0].reshape(512, 256), preferred_element_type=F32)
+        lhs = jnp.concatenate([weights(1, n), weights(2, n)], axis=1)
+        total[n] = jnp.dot(lhs, r[1:3].reshape(1024, 256), preferred_element_type=F32)
 
     for c in shares:
         c.wait_recv()
     scale = 1.0 / math.sqrt(4 * 16 * 8192)
     filter_out[...] = ((fmine[...] + fgot[1]) + (fgot[2] + fgot[3])) * scale
 
-    others.wait_recv()
+    firsts.wait_recv()
 
     def store(n):
         at = pl.ds(pl.multiple_of(1024 * n, 1024), 1024)
@@ -488,8 +503,7 @@
 
     @pl.loop(0, 8)
     def _(n):
-        lhs = jnp.concatenate([weights(1, n), weights(2, n)], axis=1)
-        out = total[n] + jnp.dot(lhs, r[1:3].reshape(1024, 256), preferred_element_type=F32)
+        out = total[n] + jnp.dot(weights(0, n), r[0].reshape(512, 256), preferred_element_type=F32)
         tok[:, pl.ds(pl.multiple_of(1024 * n, 1024), 1024)] = out.astype(BF).T
         store(n).start()
 

time: 126 us -> 124 us (0.984)
    pallas_call x1, Pallas kernels: 116 us -> 115 us  [body(): pl.pallas_call(kernel, out_shape=[jax.ShapeDtypeStruct((32, 16, 256), BF)...]
where the time goes in v2:
time: 124 us; the launch traced here: 123 us
  Pallas kernels  115 us (93%)
  local copies, waits for them, and re-layouts  6.93 us (6%)
    pallas_call x1, Pallas kernels, body(): pl.pallas_call(kernel, out_shape=[jax.ShapeDtypeStruct((32, 16, 256), BF)...  115 us
    unnamed x5, local copies, waits for them, and re-layouts  6.93 us

profile of v2, /device:TPU:0, one launch (start us, length us, event | category | flops | bytes accessed | tf_op | source)
XLA Modules:
  0.0 122.6 jit_solution(2704646844820161452)
XLA Ops:
  0.6 115.0 %shard_map.76 = (bf16[32,16,256]{2,1,0:T(8,128)(2,1)}, bf16[256,8192]{1,0:T(8,128)(2,1)}, f32[1,8192]{1,0:T(1,128)}) custom-call(bf16[256,8192]{1,0:T(8,128)(2,1)} %bitcast.4, bf16[64,1536]{1,0:T(8,128)(2,1)} %own.1, f32[3,1536]{1,0:T(4,128)} %taps.1, f32[1,8192]{1,0:T(1,128)} %h.1, bf16[32,16,256]{2,1,0:T(8,128)(2,1)} %bitcast.6), custom_call_target="tpu_custom_call" | custom-call | tf_op jit(solution)/shard_map/pallas_call | solution.py:527
  115.6 1.7 %copy.11 = bf16[1,512,256]{2,1,0:T(8,128)(2,1)} copy(bf16[1,512,256]{2,1,0:T(8,128)(2,1)} %bitcast.7) | data formatting | bytes 524288
  117.3 0.0 copy-start
  117.3 4.6 %copy.12 = bf16[1,256,8192]{2,1,0:T(8,128)(2,1)} copy(bf16[1,256,8192]{2,1,0:T(8,128)(2,1)} %bitcast.5) | data formatting | bytes 8388608
  122.0 0.0 copy-done
  122.0 0.6 copy.13
Async XLA Ops:
  117.3 4.6 %copy-start = (f32[1,8192]{1,0:T(1,128)S(1)}, f32[1,8192]{1,0:T(1,128)}, u32[]{:S(2)}) copy-start(f32[1,8192]{1,0:T(1,128)} %get-tuple-element.14) | copy-start | bytes 98308

commit v3 on v2

--- a/solution.py
+++ b/solution.py
@@ -325,13 +325,10 @@
     for fc in range(2):
         if part == 0:
             fy = (y + near) % 2
-            if len(subs) == 4:
-                piece(fy * 2 + fc, 2048, w[part, fy, fc])
-            else:
-                for sub in subs:
-                    fx = (x + sub) % 4
-                    for fz in range(4):
-                        piece(((fy * 2 + fc) * 4 + fz) * 4 + fx, 128, w[part, fy, fc, fz, fx])
+            for sub in subs:
+                fx = (x + sub) % 4
+                for fz in range(4):
+                    piece(((fy * 2 + fc) * 4 + fz) * 4 + fx, 128, w[part, fy, fc, fz, fx])
         for hop in (0, 2):
             if part == 1:
                 fz = (z + near + hop) % 4
@@ -353,7 +350,7 @@
 def kernel(
     tok_hbm, own, taps, h, cot_hbm,
     gated_out, grad_out, filter_out,
-    w, tok, acc3, p, x, u, s, tap, wide, mpad, gpad, acc, grad, pg, r, mt, z8, total, gated, fmine, fgot,
+    w, tok, acc3, p, x, u, s, tap, wide, mpad, gpad, acc, grad, pg, r, mt, z8, gated, fmine, fgot,
     put, send, recv, sib_send, sib_recv, local, a2a_send, a2a_recv, f_send, f_recv, out_sem,
 ):
     g = Gather(w, own, send, recv, sib_send, sib_recv)
@@ -405,6 +402,7 @@
         g.first(part, 1)
         g.first(part, 2, 0)
         g.go(g.sibling(part, 0, 0))
+    fill_toeplitz(h, s)
     for kind in range(2):
         for part in parts:
             g.forward(part, 1, kind)
@@ -415,34 +413,47 @@
             g.last(part, 1, kind)
         g.first(part, 2, 2)
         g.go(g.sibling(part, 0, 2))
-    fill_toeplitz(h, s)
-    for kind in range(2):
-        for part in parts:
-            g.forward(part, 2, kind, 0)
     load.wait()
-    for sub in SUBS[1:]:
+
+    def forwards(sub):
         for kind in range(2):
             for part in parts:
                 g.forward(part, 2, kind, sub)
-    def lasts(subs):
+
+    def lasts(sub):
+        for part in parts:
+            for kind in range(2):
+                g.last(part, 2, kind, sub)
+
+    def add(near, part, subs):
         for sub in subs:
-            for part in parts:
-                for kind in range(2):
-                    g.last(part, 2, kind, sub)
-
-    lasts(SUBS[:2])
-    for part in parts:
-        g.from_sibling(part, (1, 2), SUBS)
-        project(part, 1, SUBS, pos, tok, w, acc3)
-    lasts(SUBS[2:3])
-    for part in (1, 0, 2):
-        g.from_sibling(part, (0, 3, 4), SUBS[:3])
-        project(part, 0, SUBS[1:3] if part == 1 else SUBS[:3], pos, tok, w, acc3)
-    lasts(SUBS[3:])
+            g.from_sibling(part, (1, 2) if near else (0, 3, 4), (sub,))
+        project(part, near, subs, pos, tok, w, acc3)
+
+    forwards(0)
+    forwards(3)
+    add(1, 0, (0,))
+    add(1, 2, (0,))
+    forwards(1)
+    add(1, 0, (3,))
+    add(1, 2, (3,))
+    add(1, 1, (3, 1))
+    forwards(2)
+    lasts(0)
+    add(1, 0, (1, 2))
+    add(1, 2, (1, 2))
+    lasts(3)
+    add(1, 1, (0, 2))
+    add(0, 0, (0, 3))
+    lasts(1)
+    add(0, 2, (0, 3))
+    add(0, 1, (3, 1))
+    add(0, 0, (1,))
+    add(0, 2, (1,))
+    lasts(2)
     cots.start()
-    for part in parts:
-        g.from_sibling(part, (0, 3, 4), SUBS[3:])
-        project(part, 0, (0, 2) if part == 1 else SUBS[3:], pos, tok, w, acc3)
+    for part, subs in ((0, (2,)), (2, (2,)), (1, (0, 2))):
+        add(0, part, subs)
         p[part] = acc3[part].T.astype(BF).reshape(32, 16, 256)
     projs.start()
     for part in range(3):
@@ -484,29 +495,23 @@
         return w[part, n // 4, n // 2 % 2, pl.ds(n % 2 * 2, 2)].reshape(1024, 512)
 
     others.wait_recv()
+    firsts.wait_recv()
+
+    def store(n):
+        at = pl.ds(pl.multiple_of(1024 * n, 1024), 1024)
+        return pltpu.make_async_copy(tok.at[:, at], grad_out.at[:, at], out_sem.at[n])
 
     @pl.loop(0, 8)
     def _(n):
-        lhs = jnp.concatenate([weights(1, n), weights(2, n)], axis=1)
-        total[n] = jnp.dot(lhs, r[1:3].reshape(1024, 256), preferred_element_type=F32)
+        lhs = jnp.concatenate([weights(part, n) for part in parts], axis=1)
+        out = jnp.dot(lhs, r[...].reshape(1536, 256), preferred_element_type=F32)
+        tok[:, pl.ds(pl.multiple_of(1024 * n, 1024), 1024)] = out.astype(BF).T
+        store(n).start()
 
     for c in shares:
         c.wait_recv()
     scale = 1.0 / math.sqrt(4 * 16 * 8192)
     filter_out[...] = ((fmine[...] + fgot[1]) + (fgot[2] + fgot[3])) * scale
-
-    firsts.wait_recv()
-
-    def store(n):
-        at = pl.ds(pl.multiple_of(1024 * n, 1024), 1024)
-        return pltpu.make_async_copy(tok.at[:, at], grad_out.at[:, at], out_sem.at[n])
-
-    @pl.loop(0, 8)
-    def _(n):
-        out = total[n] + jnp.dot(weights(0, n), r[0].reshape(512, 256), preferred_element_type=F32)
-        tok[:, pl.ds(pl.multiple_of(1024 * n, 1024), 1024)] = out.astype(BF).T
-        store(n).start()
-
     my_gate.wait()
     gates.wait_recv()
     for e in (cots, projs, gates, firsts, others):
@@ -551,7 +556,6 @@
             pltpu.VMEM((3, 32, 16, 256), BF),
             pltpu.VMEM((256, 512), BF),
             pltpu.VMEM((32, 8, 512), F32),
-            pltpu.VMEM((8, 1024, 256), F32),
             pltpu.VMEM((32, 16, 256), BF),
             pltpu.VMEM((1, 8192), F32),
             pltpu.VMEM((4, 1, 8192), F32),
@@ -568,7 +572,7 @@
             dma((8,)),
         ],
         compiler_params=pltpu.CompilerParams(
-            collective_id=0, has_side_effects=True, vmem_limit_bytes=62 * 1024 * 1024
+            collective_id=0, has_side_effects=True, vmem_limit_bytes=46 * 1024 * 1024
         ),
     )(tokens[0], projection, short_taps, long_filters, cotangent[0].reshape(32, 16, 256))
     return gated.reshape(1, 512, 256), token_grad[None], filter_grad

time: 124 us -> 119 us (0.960)
  Pallas kernels: 115 us -> 111 us
    pallas_call x1, Pallas kernels: 115 us -> 111 us  [body(): pl.pallas_call(kernel, out_shape=[jax.ShapeDtypeStruct((32, 16, 256), BF)...]
    unnamed x5 -> x11, local copies, waits for them, and re-layouts: 6.93 us -> 6.7 us
where the time goes in v3:
time: 119 us
  Pallas kernels  111 us (93%)
  local copies, waits for them, and re-layouts  6.7 us (6%)
    pallas_call x1, Pallas kernels, body(): pl.pallas_call(kernel, out_shape=[jax.ShapeDtypeStruct((32, 16, 256), BF)...  111 us
    unnamed x11, local copies, waits for them, and re-layouts  6.7 us

profile of v3, /device:TPU:0, one launch (start us, length us, event | category | flops | bytes accessed | tf_op | source)
XLA Modules:
  0.0 118.6 jit_solution(12470705813790648508)
XLA Ops:
  0.6 0.0 copy-start
  0.6 0.9 copy-done
  1.6 0.0 copy-start.1
  1.6 0.9 copy-done.1
  2.5 0.0 copy-start.2
  2.5 0.8 copy-done.2
  3.3 0.0 copy-start.3
  3.3 0.7 copy-done.3
  4.0 111.2 %shard_map.76 = (bf16[32,16,256]{2,1,0:T(8,128)(2,1)S(1)}, bf16[256,8192]{1,0:T(8,128)(2,1)S(1)}, f32[1,8192]{1,0:T(1,128)S(1)}) custom-call(bf16[256,8192]{1,0:T(8,128)(2,1)} %bitcast.7, bf16[64,1536]{1,0:T(8,128)(2,1)S(1)} %copy-done.1, f32[3,1536]{1,0:T(4,128)S(1)} %copy-done.3, f32[1,8192]{1,0:T(1,128)S(1)} %copy-done.2, bf16[32,16,256]{2,1,0:T(8,128)(2,1)S(1)} %bitcast.5), custom_call_target="tpu_custom_call" | custom-call | tf_op jit(solution)/shard_map/pallas_call | solution.py:532
  115.2 0.7 copy.11
  115.9 2.0 %copy.12 = bf16[1,256,8192]{2,1,0:T(8,128)(2,1)} copy(bf16[1,256,8192]{2,1,0:T(8,128)(2,1)S(1)} %bitcast.4) | data formatting | bytes 8388608
  117.9 0.6 copy.13
Async XLA Ops:
  0.6 1.0 copy-start
  1.6 0.9 copy-start.1
  2.5 0.8 copy-start.2
  3.3 0.7 copy-start.3

commit v4 on v3

--- a/solution.py
+++ b/solution.py
@@ -308,10 +308,10 @@
         each_peer(lambda d: self.copy(d).start(), 31)
 
     def wait_recv(self):
-        each_peer(lambda d: self.copy(d).wait_recv())
+        each_peer(lambda d: self.copy(d).wait_recv(), 31)
 
     def wait_send(self):
-        each_peer(lambda d: self.copy(d).wait_send())
+        each_peer(lambda d: self.copy(d).wait_send(), 31)
 
 
 def project(part, near, subs, pos, tok, w, acc):
@@ -459,7 +459,9 @@
     for part in range(3):
         x[part, t] = p[part, t]
     my_cot.wait()
+    g.wait_sends()
     cots.wait_recv()
+    cots.wait_send()
     projs.wait_recv()
 
     conv_front(x, u, tap, wide, mpad, gpad)
@@ -473,9 +475,6 @@
     query_back(tap, grad, pg)
     firsts.start()
     r[0, t] = pg[0, t]
-    gates.start()
-    my_gate = pltpu.make_async_copy(gated.at[t], gated_out.at[t], local.at[2])
-    my_gate.start()
 
     filter_back(mpad, gpad, mt, z8, fmine)
     shares = []
@@ -494,6 +493,10 @@
     def weights(part, n):
         return w[part, n // 4, n // 2 % 2, pl.ds(n % 2 * 2, 2)].reshape(1024, 512)
 
+    gates.start()
+    my_gate = pltpu.make_async_copy(gated.at[t], gated_out.at[t], local.at[2])
+    my_gate.start()
+    projs.wait_send()
     others.wait_recv()
     firsts.wait_recv()
 
@@ -514,11 +517,10 @@
     filter_out[...] = ((fmine[...] + fgot[1]) + (fgot[2] + fgot[3])) * scale
     my_gate.wait()
     gates.wait_recv()
-    for e in (cots, projs, gates, firsts, others):
+    for e in (gates, firsts, others):
         e.wait_send()
     for c in shares:
         c.wait_send()
-    g.wait_sends()
 
     @pl.loop(0, 8)
     def _(n):

time: 119 us -> 117 us (0.983)
    pallas_call x1, Pallas kernels: 111 us -> 110 us  [body(): pl.pallas_call(kernel, out_shape=[jax.ShapeDtypeStruct((32, 16, 256), BF)...]
where the time goes in v4:
time: 117 us
  Pallas kernels  110 us (94%)
  local copies, waits for them, and re-layouts  6.7 us (6%)
    pallas_call x1, Pallas kernels, body(): pl.pallas_call(kernel, out_shape=[jax.ShapeDtypeStruct((32, 16, 256), BF)...  110 us
    unnamed x11, local copies, waits for them, and re-layouts  6.7 us

profile of v4, /device:TPU:0, one launch (start us, length us, event | category | flops | bytes accessed | tf_op | source)
XLA Modules:
  0.0 116.9 jit_solution(2220556907093458009)
XLA Ops:
  0.6 0.0 copy-start
  0.6 0.9 copy-done
  1.6 0.0 copy-start.1
  1.6 0.9 copy-done.1
  2.5 0.0 copy-start.2
  2.5 0.8 copy-done.2
  3.3 0.0 copy-start.3
  3.3 0.7 copy-done.3
  4.0 109.6 %shard_map.76 = (bf16[32,16,256]{2,1,0:T(8,128)(2,1)S(1)}, bf16[256,8192]{1,0:T(8,128)(2,1)S(1)}, f32[1,8192]{1,0:T(1,128)S(1)}) custom-call(bf16[256,8192]{1,0:T(8,128)(2,1)} %bitcast.7, bf16[64,1536]{1,0:T(8,128)(2,1)S(1)} %copy-done.1, f32[3,1536]{1,0:T(4,128)S(1)} %copy-done.3, f32[1,8192]{1,0:T(1,128)S(1)} %copy-done.2, bf16[32,16,256]{2,1,0:T(8,128)(2,1)S(1)} %bitcast.5), custom_call_target="tpu_custom_call" | custom-call | tf_op jit(solution)/shard_map/pallas_call | solution.py:534
  113.6 0.7 copy.11
  114.3 2.0 %copy.12 = bf16[1,256,8192]{2,1,0:T(8,128)(2,1)} copy(bf16[1,256,8192]{2,1,0:T(8,128)(2,1)S(1)} %bitcast.4) | data formatting | bytes 8388608
  116.3 0.6 copy.13
Async XLA Ops:
  0.6 1.0 copy-start
  1.6 0.9 copy-start.1
  2.5 0.8 copy-start.2
  3.3 0.7 copy-start.3
